TPU v7x, 32 devices: a whole 2x2x4 slice. The times are simulated.
32 devices in a mesh: mem: 8 (over z, x), pb: 4 (over y, core).
Axes of the slice: x: 2, y: 2, z: 4, core: 2. Of those that a mesh axis runs over, the one named last changes fastest.
Arguments:
- queries: bfloat16 [4096, 1024], P(('pb', 'mem')), may hold values from -9 to 9
- local_keys: bfloat16 [4096, 1024], P(('pb', 'mem')), may hold values from -9 to 9
- local_values: bfloat16 [4096, 1024], P(('pb', 'mem')), may hold values from -6 to 6
- memory_keys: bfloat16 [8192, 1024], P('mem'), may hold values from -11 to 11
- memory_values: bfloat16 [8192, 1024], P('mem'), may hold values from -6 to 6
- neighbour_index_rows: int32 [4096, 32], P(('pb', 'mem')), may hold values from 0 to 8191, as said below
- gate_bias: float32 [8], replicated, may hold values from -2.5 to 2.5
- out_weight: bfloat16 [1024, 1024], P('pb'), may hold values from -0.75 to 0.75
Outputs:
- layer_out: bfloat16 [4096, 1024], P(('pb', 'mem'))
Inputs may be any that keep to these rules, and one draw needn't show every extreme that they name: `neighbour_index_rows`: memory shard o holds rows o * 1024 to (o + 1) * 1024 - 1. Among the 4096 ids of one device's rows, at most 1024 fall in any one shard, and exactly 1024 fall in some shard; for each index of pb, one shard receives exactly 1024 from every device with that index. Ids of a row may repeat.
All inputs are finite; a program needn't handle non-finite values.
Results may differ from a plain program's by a relative error of at most 0.01.
Values may be sent and summed in bfloat16 or wider, within the bound.
A program may use at most 192 MiB of HBM per device.

v0:
```python
import math
import jax
import jax.numpy as jnp
from jax import lax
from jax.sharding import PartitionSpec as P


def combined_all(value, axis, join):
    pieces = jax.tree.map(lambda part: lax.all_gather(part, axis), value)
    head = jax.tree.map(lambda part: part[0], pieces)
    tail = jax.tree.map(lambda part: part[1:], pieces)
    subtotal, _ = lax.scan(lambda subtotal, share: (join(subtotal, share), None), head, tail)
    return subtotal


def join_totals(first, second):
    peak = jnp.maximum(first[0], second[0])
    return (peak, first[1] * jnp.exp(first[0] - peak) + second[1] * jnp.exp(second[0] - peak))


def slot_ranks(owners, count):
    onehot = (owners[:, None] == jnp.arange(count, dtype=jnp.int32)[None, :]).astype(jnp.int32)
    return jnp.sum(jnp.cumsum(onehot, axis=0) * onehot, axis=1) - 1


def body(
    queries,
    local_keys,
    local_values,
    memory_keys,
    memory_values,
    neighbour_index_rows,
    gate_bias,
    out_weight,
):
    shard_count = lax.axis_size("mem")
    my_shard = lax.axis_index("mem")
    row_count = queries.shape[0]
    model_width = queries.shape[1]
    head_count = gate_bias.shape[0]
    head_size = model_width // head_count
    memory_rows = memory_keys.shape[0]
    top_count = neighbour_index_rows.shape[1]
    capacity = 2 * row_count * top_count // shard_count
    group_rows = shard_count * row_count
    multiplier = head_size ** (-0.5)
    row_numbers = jnp.arange(row_count, dtype=jnp.int32)
    group_queries = lax.all_gather(queries, "mem", axis=0, tiled=True)
    query_heads = queries.reshape(row_count, head_count, head_size)
    key_local = local_keys.reshape(row_count, head_count, head_size)
    value_local = local_values.reshape(row_count, head_count, head_size)
    local_scores = (
        jnp.einsum("qhd,khd->hqk", query_heads, key_local, preferred_element_type=jnp.float32)
        * multiplier
    )
    causal = row_numbers[:, None] >= row_numbers[None, :]
    local_scores = jnp.where(causal[None], local_scores, -jnp.inf)
    local_peak = jnp.max(local_scores, axis=-1, keepdims=True)
    local_expo = jnp.exp(local_scores - local_peak)
    local_weights = (local_expo / jnp.sum(local_expo, axis=-1, keepdims=True)).astype(jnp.bfloat16)
    local_out = jnp.einsum(
        "hqk,khd->qhd", local_weights, value_local, preferred_element_type=jnp.float32
    )
    key_head_count = memory_keys.reshape(memory_rows, head_count, head_size)
    block = math.gcd(group_rows, 512)

    def block_stats(query_tile_block):
        reshaped_tensor = query_tile_block.reshape(block, head_count, head_size)
        logit_scores = (
            jnp.einsum(
                "bvt,yvt->bvy", reshaped_tensor, key_head_count, preferred_element_type=jnp.float32
            )
            * multiplier
        )
        block_peak = jnp.max(logit_scores, axis=2)
        return (block_peak, jnp.sum(jnp.exp(logit_scores - block_peak[:, :, None]), axis=2))

    peaks, totals = lax.map(
        block_stats, group_queries.reshape(group_rows // block, block, model_width)
    )
    peaks = peaks.reshape(group_rows, head_count)
    totals = totals.reshape(group_rows, head_count)
    global_peak, global_total = combined_all((peaks, totals), "mem", join_totals)
    source_queries = group_queries.reshape(shard_count, row_count, head_count, head_size)
    source_peaks = global_peak.reshape(shard_count, row_count, head_count)
    flat_ids = neighbour_index_rows.reshape(-1)
    entry_row_list = jnp.arange(row_count * top_count, dtype=jnp.int32) // top_count
    owners = flat_ids // memory_rows
    ranks = slot_ranks(owners, shard_count)
    codes = entry_row_list * memory_rows + flat_ids % memory_rows
    slots = owners * capacity + ranks
    requests = (
        jnp.full((shard_count * capacity,), -1, jnp.int32)
        .at[slots]
        .set(codes)
        .reshape(shard_count, capacity)
    )
    slot_owner_row = (
        jnp.full((shard_count * capacity,), -1, jnp.int32).at[slots].set(entry_row_list)
    )
    codes = lax.all_to_all(requests, "mem", split_axis=0, concat_axis=0, tiled=True)
    valid = codes >= 0
    safe = jnp.where(valid, codes, 0)
    offsets = safe % memory_rows
    local_rows = jnp.where(valid, safe // memory_rows, -1)
    slot_width = codes.shape[1]
    picked_keys = memory_keys[offsets].reshape(codes.shape[0], slot_width, head_count, head_size)
    values = memory_values[offsets]

    def score_source(inputs):
        query_block, key_block, rows_here, peak_block = inputs
        full = (
            jnp.einsum("qhd,chd->hqc", query_block, key_block, preferred_element_type=jnp.float32)
            * multiplier
        )
        hit = rows_here[None, :] == row_numbers[:, None]
        scores = jnp.sum(jnp.where(hit[None], full, 0.0), axis=1)
        peak_here = jnp.sum(jnp.where(hit[:, :, None], peak_block[:, None, :], 0.0), axis=0)
        weight_here = jnp.exp(scores.T - peak_here)
        return jnp.where((rows_here >= 0)[:, None], weight_here, 0.0).astype(jnp.bfloat16)

    weights = lax.map(score_source, (source_queries, picked_keys, local_rows, source_peaks))
    weights, values, local_rows = (weights, values, local_rows)
    values, weights = (
        lax.all_to_all(values, "mem", split_axis=0, concat_axis=0, tiled=True),
        lax.all_to_all(weights, "mem", split_axis=0, concat_axis=0, tiled=True),
    )
    flat_values = values.reshape(shard_count * capacity, head_count, head_size)
    flat_weights = weights.reshape(shard_count * capacity, head_count)
    hit = slot_owner_row[None, :] == row_numbers[:, None]
    scaled = jnp.where(hit[None], flat_weights.T[:, None, :], jnp.zeros((), jnp.bfloat16))
    numerator = jnp.einsum("hqs,shd->qhd", scaled, flat_values, preferred_element_type=jnp.float32)
    denominator = jnp.dot(
        hit.astype(jnp.bfloat16), flat_weights, preferred_element_type=jnp.float32
    )
    own_total = lax.dynamic_slice_in_dim(global_total, my_shard * row_count, row_count, 0)
    background = top_count / (memory_rows * shard_count) * own_total
    memory_out = numerator / (denominator + background)[:, :, None]
    gate = jax.nn.sigmoid(gate_bias)[None, :, None]
    mixed = (
        (gate * memory_out + (1.0 - gate) * local_out)
        .reshape(row_count, model_width)
        .astype(jnp.bfloat16)
    )
    result = jnp.dot(
        mixed,
        lax.all_gather(out_weight, "pb", axis=0, tiled=True),
        preferred_element_type=jnp.float32,
    )
    return result.astype(jnp.bfloat16)


def solution(mesh):
    in_specs = (
        P(("pb", "mem"), None),
        P(("pb", "mem"), None),
        P(("pb", "mem"), None),
        P("mem", None),
        P("mem", None),
        P(("pb", "mem"), None),
        P(),
        P("pb", None),
    )
    out_specs = P(("pb", "mem"), None)
    return jax.shard_map(body, mesh=mesh, in_specs=in_specs, out_specs=out_specs, check_vma=False)
```

profile of v0, /device:TPU:0, one launch (start us, length us, event | category | flops | bytes accessed | tf_op | source)
XLA Modules:
  0.0 718.5 jit_solution(11344651262773590090)
XLA Ops:
  7.4 0.7 all-gather.3.cloned.1.call-update
  8.1 0.8 copy.62
  9.2 2.3 reduce-window.6
  12.4 16.1 %scatter_custom_fusion = s32[8192]{0:T(1024)} fusion(s32[4096]{0:T(1024)S(1)} %bitcast.179, s32[4096]{0:T(1024)S(1)} %get-tuple-element.207, s32[]{:T(128)} %constant.123.clone.1), kind=kCustom, calls=%fused_computation.112 | custom fusion | bytes 32772 | tf_op jit(solution)/shard_map/scatter | solution.py:95
  28.5 7.3 %all-to-all-start = ((s32[8,1,1024]{2,1,0:T(1,128)}), s32[8,1,1024]{2,1,0:T(1,128)S(1)}, u32[]{:S(2)}, u32[]{:S(2)}) async-start(s32[8,1,1024]{2,1,0:T(1,128)} %bitcast.9), calls=%async_computation | async-start | bytes 65536 | tf_op jit(solution)/shard_map/all_to_all | solution.py:101
  35.8 4.0 copy.67
  39.7 3.9 copy.69
  43.8 42.5 %gather_fusion.1 = bf16[8192,1024]{1,0:T(8,128)(2,1)} fusion(bf16[1024,1024]{1,0:T(8,128)(2,1)} %param.17, s32[8192]{0:T(1024)S(1)} %broadcast_clamp_fusion), kind=kCustom, calls=%fused_computation.1 | custom fusion | bytes 33587200 | tf_op jit(solution)/shard_map/gather | solution.py:107
  86.3 15.6 %copy.87 = bf16[1024,8,8,128]{3,2,1,0:T(8,128)(2,1)} copy(bf16[1024,8,8,128]{3,1,2,0:T(8,128)(2,1)} %bitcast.161) | data formatting | bytes 33554432
  102.0 23.2 %while.35 = (s32[]{:T(128)}, f32[2,512,8]{1,2,0:T(8,128)S(1)}, f32[2,512,8]{1,2,0:T(8,128)S(1)}, bf16[2,512,1024]{2,1,0:T(8,128)(2,1)}, bf16[1024,8,128]{2,0,1:T(8,128)(2,1)}, /*index=5*/s32[]{:T(128)}) while((s32[]{:T(128)}, f32[2,512,8]{1,2,0:T(8,128)S(1)}, f32[2,512,8]{1,2,0:T(8,128)S(1)}, bf16[2,512,1024]{2,1,0:T(8,128)(2,1)}, ...), condition=%wide.region_8.9_spmd, body=%wide.region_5.8_spmd.sunk | while | flops 1094705152 | bytes 41009228 | solution.py:78
  102.0 2.3 constant_dynamic-slice_fusion.8
  104.3 1.5 copy.106
  105.8 4.2 bitcast_reduce_fusion.2
  110.1 3.5 fusion.76
  113.6 2.3 constant_dynamic-slice_fusion.8
  115.9 1.5 copy.106
  117.4 4.2 bitcast_reduce_fusion.2
  121.6 3.5 fusion.76
  125.2 31.4 %all_gather.14 = f32[8,1024,8]{1,2,0:T(8,128)S(1)} all-gather(f32[1,1024,8]{1,2,0:T(8,128)S(1)} %bitcast.177), channel_id=1, replica_groups=mesh['mem'=8,'pb'=4] {'mem'}, dimensions={0}, use_global_device_ids=true | all-gather | bytes 294912 | tf_op jit(solution)/shard_map/all_gather | solution.py:9
  156.6 30.7 %all_gather.13 = f32[8,1024,8]{1,2,0:T(8,128)S(1)} all-gather(f32[1,1024,8]{1,2,0:T(8,128)S(1)} %bitcast.176), channel_id=1, replica_groups=mesh['mem'=8,'pb'=4] {'mem'}, dimensions={0}, use_global_device_ids=true | all-gather | bytes 294912 | tf_op jit(solution)/shard_map/all_gather | solution.py:9
  187.8 3.6 copy.86
  191.4 43.2 %while.37 = (s32[]{:T(128)}, bf16[8,1024,8]{1,2,0:T(8,128)(2,1)}, s32[8,1024]{1,0:T(8,128)S(1)}, bf16[8,128,8,128]{3,2,1,0:T(8,128)(2,1)}, bf16[8,1024,8,128]{3,...) while((s32[]{:T(128)}, bf16[8,1024,8]{1,2,0:T(8,128)(2,1)}, ...), condition=%wide.region_14.15_spmd.clone, body=%wide.region_11.14_spmd.clone.sunk | while | flops 273818624 | bytes 7658077 | solution.py:122
  191.4 1.7 constant_dynamic-slice_fusion.10
  193.2 1.0 constant_dynamic-slice_fusion.11
  194.2 1.2 select_reduce_fusion.5
  195.5 0.6 select_reduce_fusion.4
  196.8 1.7 constant_dynamic-slice_fusion.10
  198.6 1.0 constant_dynamic-slice_fusion.11
  199.6 1.2 select_reduce_fusion.5
  200.9 0.6 select_reduce_fusion.4
  202.2 1.7 constant_dynamic-slice_fusion.10
  204.0 1.0 constant_dynamic-slice_fusion.11
  205.0 1.2 select_reduce_fusion.5
  206.3 0.6 select_reduce_fusion.4
  207.6 1.7 constant_dynamic-slice_fusion.10
  209.4 1.0 constant_dynamic-slice_fusion.11
  210.4 1.2 select_reduce_fusion.5
  213.1 1.7 constant_dynamic-slice_fusion.10
  214.8 1.0 constant_dynamic-slice_fusion.11
  215.8 1.2 select_reduce_fusion.5
  217.1 0.6 select_reduce_fusion.4
  218.5 1.7 constant_dynamic-slice_fusion.10
  220.2 1.0 constant_dynamic-slice_fusion.11
  221.2 1.2 select_reduce_fusion.5
  222.5 0.6 select_reduce_fusion.4
  223.9 1.7 constant_dynamic-slice_fusion.10
  225.6 1.0 constant_dynamic-slice_fusion.11
  226.6 1.2 select_reduce_fusion.5
  229.3 1.7 constant_dynamic-slice_fusion.10
  231.0 1.0 constant_dynamic-slice_fusion.11
  232.0 1.2 select_reduce_fusion.5
  234.6 5.4 all-to-all-start.2
  239.9 35.4 %gather_fusion = bf16[8192,1024]{1,0:T(8,128)(2,1)} fusion(bf16[1024,1024]{1,0:T(8,128)(2,1)S(1)} %copy-done, s32[8192]{0:T(1024)S(1)} %broadcast_clamp_fusion), kind=kCustom, calls=%fused_computation | custom fusion | bytes 33587200 | tf_op jit(solution)/shard_map/gather | solution.py:108
  275.4 21.6 %copy.65 = bf16[8,1024,1024]{1,2,0:T(8,128)(2,1)} copy(bf16[8,1024,1024]{2,1,0:T(8,128)(2,1)} %bitcast.160) | data formatting | bytes 33554432 | tf_op jit(solution)/shard_map/gather | solution.py:108
  297.0 6.1 all-to-all-start.1
  303.7 15.7 %scatter_custom_fusion.1 = s32[8192]{0:T(1024)S(1)} fusion(s32[4096]{0:T(1024)} %bitcast.180, s32[4096]{0:T(1024)S(1)} %add_select_fusion.2, s32[]{:T(128)} %constant.123.clone.1), kind=kCustom, calls=%fused_computation.110 | custom fusion | bytes 33280 | tf_op jit(solution)/shard_map/scatter | solution.py:99
  319.4 0.8 copy.78
  321.3 0.7 convolution_add_fusion
  322.1 331.0 %all-to-all-done.1 = bf16[8,1024,1024]{1,2,0:T(8,128)(2,1)} async-done(((bf16[8,1024,1024]{1,2,0:T(8,128)(2,1)}), bf16[8,1024,1024]{1,2,0:T(8,128)(2,1)}, u32[]{:S(2)}, u32[]{:S(2)}) %all-to-all-start.1) | async-done | bytes 16777248 | tf_op jit(solution)/shard_map/all_to_all | solution.py:125
  653.1 18.7 %copy.66 = bf16[8,1024,1024]{1,0,2:T(8,128)(2,1)} copy(bf16[8,1024,1024]{1,2,0:T(8,128)(2,1)} %all-to-all-done.1) | data formatting | bytes 33554432 | tf_op jit(solution)/shard_map/all_to_all | solution.py:125
  671.8 25.6 %reshape.338 = bf16[8192,8,128]{0,2,1:T(8,128)(2,1)} reshape(bf16[8,1024,1024]{1,0,2:T(8,128)(2,1)} %copy.66) | data formatting | bytes 33554432 | tf_op jit(solution)/shard_map/reshape | solution.py:128
  697.4 9.2 %fusion.29 = f32[128,8,128]{0,2,1:T(8,128)} fusion(bf16[8192,8,128]{0,2,1:T(8,128)(2,1)} %reshape.338, pred[128,8192]{1,0:T(8,128)(4,1)S(1)} %iota_compare_fusion.1, bf16[8,8192]{1,0:T(8,128)(2,1)S(1)} %bitcast.173, f32[128,8]{0,1:T(8,128)S(1)} %convolution_add_fusion, f32[8]{0:T(128)S(1)} %get-tuple-element.202), kind=kOutput, calls=%fused_computation.52 | convolution fusion | flops 2156134400 | bytes 18485280 | tf_op jit(solution)/shard_map/hqs,shd->qhd/dot_general | solution.py:132
  706.5 1.7 fusion.25
  708.3 2.8 convolution_convert_fusion
  (112 shorter events, 12.2 us)
Async XLA Ops:
  7.4 232.6 %copy-start = (bf16[1024,1024]{1,0:T(8,128)(2,1)S(1)}, bf16[1024,1024]{1,0:T(8,128)(2,1)}, u32[]{:S(2)}) copy-start(bf16[1024,1024]{1,0:T(8,128)(2,1)} %param.18) | copy-start | bytes 6291460
  7.4 94.7 %all-gather.3.cloned.1.call-start = ((), (), s32[]{:S(2)}) async-start(), calls=%async_computation.3 | async-start | bytes 2359296 | tf_op jit(solution)/shard_map/all_gather | solution.py:48
  12.4 31.3 %copy-start.5 = (s32[4096,1]{0,1:T(1,128)}, s32[4096,1]{0,1:T(1,128)S(1)}, u32[]{:S(2)}) copy-start(s32[4096,1]{0,1:T(1,128)S(1)} %compare_select_fusion.4) | copy-start | bytes 49156
  28.5 15.2 %all-to-all-start = ((s32[8,1,1024]{2,1,0:T(1,128)}), s32[8,1,1024]{2,1,0:T(1,128)S(1)}, u32[]{:S(2)}, u32[]{:S(2)}) async-start(s32[8,1,1024]{2,1,0:T(1,128)} %bitcast.9), calls=%async_computation | async-start | bytes 65536 | tf_op jit(solution)/shard_map/all_to_all | solution.py:101
  234.6 62.4 %all-to-all-start.2 = ((bf16[8,1024,8]{1,2,0:T(8,128)(2,1)}), bf16[8,1024,8]{1,2,0:T(8,128)(2,1)S(1)}, u32[]{:S(2)}, u32[]{:S(2)}) async-start(bf16[8,1024,8]{1,2,0:T(8,128)(2,1)} %get-tuple-element.101), calls=%async_computation.2 | async-start | bytes 262144 | tf_op jit(solution)/shard_map/all_to_all | solution.py:126
  296.9 22.5 %copy-start.3 = (bf16[128,1024]{1,0:T(8,128)(2,1)S(1)}, bf16[128,1024]{1,0:T(8,128)(2,1)}, u32[]{:S(2)}) copy-start(bf16[128,1024]{1,0:T(8,128)(2,1)} %param.16) | copy-start | bytes 786436
  296.9 23.3 %copy-start.4 = (bf16[128,1024]{1,0:T(8,128)(2,1)S(1)}, bf16[128,1024]{1,0:T(8,128)(2,1)}, u32[]{:S(2)}) copy-start(bf16[128,1024]{1,0:T(8,128)(2,1)} %param.14) | copy-start | bytes 786436
  296.9 23.3 %copy-start.6 = (bf16[128,1024]{1,0:T(8,128)(2,1)S(1)}, bf16[128,1024]{1,0:T(8,128)(2,1)}, u32[]{:S(2)}) copy-start(bf16[128,1024]{1,0:T(8,128)(2,1)} %param.15) | copy-start | bytes 786436
  296.9 23.8 %copy-start.7 = (f32[8]{0:T(128)S(1)}, f32[8]{0:T(128)}, u32[]{:S(2)}) copy-start(f32[8]{0:T(128)} %param.20) | copy-start | bytes 100
  297.0 356.1 %all-to-all-start.1 = ((bf16[8,1024,1024]{1,2,0:T(8,128)(2,1)}), bf16[8,1024,1024]{1,2,0:T(8,128)(2,1)}, u32[]{:S(2)}, u32[]{:S(2)}) async-start(bf16[8,1024,1024]{1,2,0:T(8,128)(2,1)} %copy.65), calls=%async_computation.1 | async-start | bytes 33554432 | tf_op jit(solution)/shard_map/all_to_all | solution.py:125
  303.1 405.2 %all-gather.5.cloned.1.call-start = ((), (), s32[]{:S(2)}) async-start(), calls=%async_computation.4 | async-start | bytes 2621440 | tf_op jit(solution)/shard_map/all_gather | solution.py:147
  320.6 351.2 %copy-start.2 = (f32[8,128,128]{1,2,0:T(8,128)}, f32[8,128,128]{1,2,0:T(8,128)S(1)}, u32[]{:S(2)}) copy-start(f32[8,128,128]{1,2,0:T(8,128)S(1)} %fusion.21) | copy-start | bytes 1572868
  697.4 13.7 %copy-start.1 = (bf16[1024,1024]{1,0:T(8,128)(2,1)S(1)}, bf16[1024,1024]{1,0:T(8,128)(2,1)}, u32[]{:S(2)}) copy-start(bf16[1024,1024]{1,0:T(8,128)(2,1)} %param.18) | copy-start | bytes 6291460
Sparse Core Ops, SparseCore 0:
  10.3 51.9 all-gather.2
Sparse Core Ops, SparseCore 1:
  305.1 23.8 all-gather.4
where the time goes:
time: 721 us; the launch traced here: 719 us
  waiting for transfers between devices  332 us (46%)
  local copies, waits for them, and re-layouts  235 us (33%)
  blocking collectives  62.1 us (9%)
  matrix products  32.6 us (5%)
  other arithmetic  21.9 us (3%)
  starting transfers between devices  18.8 us (3%)
  between operations  15.1 us (2%)
    all_to_all x1, waiting for transfers between devices, body(): lax.all_to_all(values, 'mem', split_axis=0, concat_axis=0, tiled=True)  331 us
    all_gather x2, blocking collectives, combined_all(): pieces = jax.tree.map(lambda part: lax.all_gather(part, axis), value)  62.1 us
    gather x2, local copies, waits for them, and re-layouts, body(): values = memory_values[offsets]  57 us
    gather x1, local copies, waits for them, and re-layouts, body(): memory_keys[offsets]  42.5 us
    reshape x1, local copies, waits for them, and re-layouts, body(): flat_values = values.reshape(shard_count * capacity, head_count, head_size)  25.6 us
    unnamed x20, local copies, waits for them, and re-layouts  24 us
    dynamic_slice x24, local copies, waits for them, and re-layouts, body(): lax.map(score_source, (source_queries, picked_keys, local_rows, source_pe...  21.7 us
    all_to_all x1, local copies, waits for them, and re-layouts, body(): lax.all_to_all(values, 'mem', split_axis=0, concat_axis=0, tiled=True)  18.7 us
  transfers between devices with their start and end apart: 5, of which 1 were waited for; matrix products, arithmetic and copies ran while one was open for 30% of the time, Pallas kernels for 0%

commit v1 on v0

--- a/solution.py
+++ b/solution.py
@@ -3,6 +3,40 @@
 import jax.numpy as jnp
 from jax import lax
 from jax.sharding import PartitionSpec as P
+
+
+def _push_words(field, array_axis, xin):
+    vec_out = field.shape
+    t_next = field.reshape(
+        *vec_out[:array_axis], xin, vec_out[array_axis] // xin, *vec_out[array_axis + 1 :]
+    )
+    near = jnp.moveaxis(t_next, array_axis, 0)
+    return near
+
+
+def _rest_members_all(u_in, out_dim):
+    u_in = jnp.moveaxis(u_in, 0, out_dim)
+    mixed_arr = u_in.shape
+    g_now = u_in.reshape(
+        *mixed_arr[:out_dim], mixed_arr[out_dim] * mixed_arr[out_dim + 1], *mixed_arr[out_dim + 2 :]
+    )
+    return g_now
+
+
+def part_the_halves(vector, lane_axis, array_in, x_local):
+    small = lax.axis_index(lane_axis)
+    parts_out = lax.axis_size(lane_axis)
+    side_arr, u_next = (parts_out, small)
+    n_now = _push_words(vector, array_in, side_arr)
+    x_next = n_now
+    for k0 in range(1, side_arr):
+        earlier, res = ((u_next + k0) % side_arr, (u_next - k0) % side_arr)
+        block_now = lax.dynamic_index_in_dim(n_now, earlier, 0)
+        newest = tuple(((dev_j, (dev_j + k0) % side_arr) for dev_j in range(side_arr)))
+        latest = lax.ppermute(block_now, lane_axis, newest)
+        x_next = lax.dynamic_update_slice_in_dim(x_next, latest, res, axis=0)
+    current_value = _rest_members_all(x_next, x_local)
+    return current_value
 
 
 def combined_all(value, axis, join):
@@ -122,7 +156,7 @@
     weights = lax.map(score_source, (source_queries, picked_keys, local_rows, source_peaks))
     weights, values, local_rows = (weights, values, local_rows)
     values, weights = (
-        lax.all_to_all(values, "mem", split_axis=0, concat_axis=0, tiled=True),
+        part_the_halves(values, "mem", 0, 0),
         lax.all_to_all(weights, "mem", split_axis=0, concat_axis=0, tiled=True),
     )
     flat_values = values.reshape(shard_count * capacity, head_count, head_size)

time: 721 us -> 657 us (0.911)
  waiting for transfers between devices: 332 us -> 153 us
  blocking collectives: 62.1 us -> 191 us
  local copies, waits for them, and re-layouts: 235 us -> 206 us
  starting transfers between devices: 18.8 us -> 31.8 us
    all_to_all x1 -> x0, waiting for transfers between devices: 331 us -> none  [body(): lax.all_to_all(values, 'mem', split_axis=0, concat_axis=0, tiled=True)]
    ppermute x0 -> x7, waiting for transfers between devices: none -> 149 us  [part_the_halves(): latest = lax.ppermute(block_now, lane_axis, newest)]
    all_gather x2, blocking collectives: 62.1 us -> 191 us  [combined_all(): pieces = jax.tree.map(lambda part: lax.all_gather(part, axis), value)]
    reshape x1 -> x0, local copies, waits for them, and re-layouts: 25.6 us -> none  [body(): flat_values = values.reshape(shard_count * capacity, head_count, head_size)]
    dynamic_update_slice x0 -> x7, local copies, waits for them, and re-layouts: none -> 21.7 us  [part_the_halves(): x_next = lax.dynamic_update_slice_in_dim(x_next, latest, res, axis=0)]
    gather x2 -> x1, local copies, waits for them, and re-layouts: 57 us -> 35.4 us  [body(): values = memory_values[offsets]]
    all_to_all x1 -> x0, local copies, waits for them, and re-layouts: 18.7 us -> none  [body(): lax.all_to_all(values, 'mem', split_axis=0, concat_axis=0, tiled=True)]
    ppermute x0 -> x7, starting transfers between devices: none -> 18.5 us  [part_the_halves(): latest = lax.ppermute(block_now, lane_axis, newest)]
  transfers between devices with their start and end apart: 5 -> 11, of which waited for: 1 -> 3; matrix products, arithmetic and copies ran while one was open for 30% -> 40% of each run, Pallas kernels for 0% -> 0%
where the time goes in v1:
time: 657 us; the launch traced here: 655 us
  local copies, waits for them, and re-layouts  206 us (31%)
  blocking collectives  191 us (29%)
  waiting for transfers between devices  153 us (23%)
  matrix products  36.2 us (6%)
  starting transfers between devices  31.8 us (5%)
  other arithmetic  23.7 us (4%)
  between operations  13.6 us (2%)
    all_gather x2, blocking collectives, combined_all(): pieces = jax.tree.map(lambda part: lax.all_gather(part, axis), value)  191 us
    ppermute x7, waiting for transfers between devices, part_the_halves(): latest = lax.ppermute(block_now, lane_axis, newest)  149 us
    unnamed x25, local copies, waits for them, and re-layouts  39.1 us
    gather x1, local copies, waits for them, and re-layouts, body(): values = memory_values[offsets]  35.4 us
    gather x1, local copies, waits for them, and re-layouts, body(): memory_keys[offsets]  35.4 us
    dynamic_slice x24, local copies, waits for them, and re-layouts, body(): lax.map(score_source, (source_queries, picked_keys, local_rows, source_pe...  21.7 us
    dynamic_update_slice x7, local copies, waits for them, and re-layouts, part_the_halves(): x_next = lax.dynamic_update_slice_in_dim(x_next, latest, res, axis=0)  21.7 us
    ppermute x7, starting transfers between devices, part_the_halves(): latest = lax.ppermute(block_now, lane_axis, newest)  18.5 us
  transfers between devices with their start and end apart: 11, of which 3 were waited for; matrix products, arithmetic and copies ran while one was open for 40% of the time, Pallas kernels for 0%

profile of v1, /device:TPU:0, one launch (start us, length us, event | category | flops | bytes accessed | tf_op | source)
XLA Modules:
  0.0 655.2 jit_solution(14052983296889186038)
XLA Ops:
  8.4 2.3 reduce-window.6
  11.6 16.1 %scatter_custom_fusion = s32[8192]{0:T(1024)} fusion(s32[4096]{0:T(1024)S(1)} %bitcast.199, s32[4096]{0:T(1024)S(1)} %get-tuple-element.214, s32[]{:T(128)} %constant.215.clone.1), kind=kCustom, calls=%fused_computation.120 | custom fusion | bytes 32772 | tf_op jit(solution)/shard_map/scatter | solution.py:129
  27.7 7.3 %all-to-all-start = ((s32[8,1,1024]{2,1,0:T(1,128)}), s32[8,1,1024]{2,1,0:T(1,128)S(1)}, u32[]{:S(2)}, u32[]{:S(2)}) async-start(s32[8,1,1024]{2,1,0:T(1,128)} %bitcast.9), calls=%async_computation | async-start | bytes 65536 | tf_op jit(solution)/shard_map/all_to_all | solution.py:135
  35.7 1.3 broadcast_subtract_fusion
  36.9 1.3 fusion.22
  39.8 1.9 all-to-all-done
  41.9 35.4 %gather_fusion = bf16[8192,1024]{1,0:T(8,128)(2,1)} fusion(bf16[1024,1024]{1,0:T(8,128)(2,1)S(1)} %copy-done, s32[8192]{0:T(1024)S(1)} %broadcast_clamp_fusion), kind=kCustom, calls=%fused_computation | custom fusion | bytes 33587200 | tf_op jit(solution)/shard_map/gather | solution.py:142
  77.3 11.0 %dynamic-slice_bitcast_fusion.1 = (bf16[1,1,1024,1024]{3,2,0,1:T(8,128)(2,1)}, bf16[1,1,1024,1024]{3,2,0,1:T(8,128)(2,1)}, bf16[1,1,1024,1024]{3,2,0,1:T(8,128)(...) fusion(bf16[8,1024,1024]{2,1,0:T(8,128)(2,1)} %bitcast.176, ...), kind=kLoop, calls=%fused_computation.41 | loop fusion | bytes 29360156 | tf_op jit(solution)/shard_map/jit(dynamic_index_in_dim)/dynamic_slice | solution.py:34
  88.8 15.5 %scatter_custom_fusion.1 = s32[8192]{0:T(1024)S(1)} fusion(s32[4096]{0:T(1024)S(1)} %bitcast.200, s32[4096]{0:T(1024)S(1)} %add_select_fusion.2, s32[]{:T(128)} %constant.215.clone.1), kind=kCustom, calls=%fused_computation.118 | custom fusion | bytes 32772 | tf_op jit(solution)/shard_map/scatter | solution.py:133
  104.4 2.6 copy.65
  106.9 3.9 copy.67
  111.7 1.2 collective-permute-start.1
  112.9 2.4 collective-permute-start.2
  115.3 1.6 collective-permute-start.3
  116.9 2.2 collective-permute-start.4
  119.6 35.4 %gather_fusion.1 = bf16[8192,1024]{1,0:T(8,128)(2,1)} fusion(bf16[1024,1024]{1,0:T(8,128)(2,1)S(1)} %copy-done.2, s32[8192]{0:T(1024)S(1)} %broadcast_clamp_fusion), kind=kCustom, calls=%fused_computation.1 | custom fusion | bytes 33587200 | tf_op jit(solution)/shard_map/gather | solution.py:141
  155.0 15.6 %copy.87 = bf16[1024,8,8,128]{3,2,1,0:T(8,128)(2,1)} copy(bf16[1024,8,8,128]{3,1,2,0:T(8,128)(2,1)} %bitcast.180) | data formatting | bytes 33554432
  170.7 1.5 collective-permute-start.5
  172.2 3.1 constant_dynamic-update-slice_fusion.6
  175.3 9.2 %collective-permute-start.6 = (bf16[1,1,1024,1024]{3,2,0,1:T(8,128)(2,1)}, bf16[1,1,1024,1024]{3,2,0,1:T(8,128)(2,1)}, u32[]{:S(2)}, u32[]{:S(2)}) collective-permute-start(bf16[1,1,1024,1024]{3,2,0,1:T(8,128)(2,1)} %get-tuple-element.207), channel_id=1, source_target_pairs={{0,28},{4,0},{8,4},{12,8},{16,12},{20,16},{24,20},{28,24},{1,29},{... | collective-permute-start | bytes 6291464 | tf_op jit(solution)/shard_map/ppermute | solution.py:36
  184.5 3.1 constant_dynamic-update-slice_fusion.5
  187.6 129.5 %collective-permute-done.2 = bf16[1,1,1024,1024]{3,2,0,1:T(8,128)(2,1)} collective-permute-done((bf16[1,1,1024,1024]{3,2,0,1:T(8,128)(2,1)}, bf16[1,1,1024,1024]{3,2,0,1:T(8,128)(2,1)}, u32[]{:S(2)}, u32[]{:S(2)}) %collective-permute-start.2) | collective-permute-done | bytes 2097184 | tf_op jit(solution)/shard_map/ppermute | solution.py:36
  317.1 3.1 constant_dynamic-update-slice_fusion.4
  320.2 19.8 %collective-permute-done.3 = bf16[1,1,1024,1024]{3,2,0,1:T(8,128)(2,1)} collective-permute-done((bf16[1,1,1024,1024]{3,2,0,1:T(8,128)(2,1)}, bf16[1,1,1024,1024]{3,2,0,1:T(8,128)(2,1)}, u32[]{:S(2)}, u32[]{:S(2)}) %collective-permute-start.3) | collective-permute-done | bytes 2097184 | tf_op jit(solution)/shard_map/ppermute | solution.py:36
  340.0 3.2 constant_dynamic-update-slice_fusion.3
  343.1 3.1 constant_dynamic-update-slice_fusion.2
  346.2 19.3 %while.35 = (s32[]{:T(128)}, f32[2,512,8]{1,2,0:T(8,128)S(1)}, f32[2,512,8]{1,2,0:T(8,128)S(1)}, bf16[2,512,1024]{2,1,0:T(8,128)(2,1)}, bf16[1024,8,128]{2,0,1:T(8,128)(2,1)}, /*index=5*/s32[]{:T(128)}) while((s32[]{:T(128)}, f32[2,512,8]{1,2,0:T(8,128)S(1)}, f32[2,512,8]{1,2,0:T(8,128)S(1)}, bf16[2,512,1024]{2,1,0:T(8,128)(2,1)}, ...), condition=%wide.region_8.9_spmd, body=%wide.region_5.8_spmd.sunk | while | flops 1094705152 | bytes 41009236 | solution.py:112
  346.2 1.3 constant_dynamic-slice_fusion.8
  348.1 4.2 bitcast_reduce_fusion.2
  352.3 3.5 fusion.82
  355.9 1.3 constant_dynamic-slice_fusion.8
  357.7 4.2 bitcast_reduce_fusion.2
  361.9 3.5 fusion.82
  365.5 160.1 %all_gather.13 = f32[8,1024,8]{1,2,0:T(8,128)S(1)} all-gather(f32[1,1024,8]{1,2,0:T(8,128)S(1)} %bitcast.196), channel_id=1, replica_groups=mesh['mem'=8,'pb'=4] {'mem'}, dimensions={0}, use_global_device_ids=true | all-gather | bytes 294912 | tf_op jit(solution)/shard_map/all_gather | solution.py:43
  525.6 30.7 %all_gather.14 = f32[8,1024,8]{1,2,0:T(8,128)S(1)} all-gather(f32[1,1024,8]{1,2,0:T(8,128)S(1)} %bitcast.197), channel_id=1, replica_groups=mesh['mem'=8,'pb'=4] {'mem'}, dimensions={0}, use_global_device_ids=true | all-gather | bytes 294912 | tf_op jit(solution)/shard_map/all_gather | solution.py:43
  556.4 3.5 copy.86
  560.3 43.2 %while.37 = (s32[]{:T(128)}, bf16[8,1024,8]{1,2,0:T(8,128)(2,1)}, s32[8,1024]{1,0:T(8,128)S(1)}, bf16[8,128,8,128]{3,2,1,0:T(8,128)(2,1)}, bf16[8,1024,8,128]{3,...) while((s32[]{:T(128)}, bf16[8,1024,8]{1,2,0:T(8,128)(2,1)}, ...), condition=%wide.region_14.15_spmd.clone, body=%wide.region_11.14_spmd.clone.sunk | while | flops 273818624 | bytes 7657577 | solution.py:156
  561.2 1.7 constant_dynamic-slice_fusion.10
  562.9 1.0 constant_dynamic-slice_fusion.11
  563.9 1.2 select_reduce_fusion.5
  566.6 1.7 constant_dynamic-slice_fusion.10
  568.3 1.0 constant_dynamic-slice_fusion.11
  569.3 1.2 select_reduce_fusion.5
  571.9 1.7 constant_dynamic-slice_fusion.10
  573.7 1.0 constant_dynamic-slice_fusion.11
  574.7 1.2 select_reduce_fusion.5
  577.3 1.7 constant_dynamic-slice_fusion.10
  580.1 1.2 select_reduce_fusion.5
  582.7 1.7 constant_dynamic-slice_fusion.10
  584.5 1.0 constant_dynamic-slice_fusion.11
  585.4 1.2 select_reduce_fusion.5
  588.1 1.7 constant_dynamic-slice_fusion.10
  590.8 1.2 select_reduce_fusion.5
  593.5 1.7 constant_dynamic-slice_fusion.10
  596.2 1.2 select_reduce_fusion.5
  598.9 1.7 constant_dynamic-slice_fusion.10
  601.6 1.2 select_reduce_fusion.5
  603.5 6.0 all-to-all-start.1
  609.5 3.1 constant_dynamic-update-slice_fusion.1
  612.5 3.1 constant_dynamic-update-slice_fusion
  615.6 15.6 %copy.85 = bf16[1024,8,8,128]{3,2,1,0:T(8,128)(2,1)} copy(bf16[1024,8,8,128]{3,1,2,0:T(8,128)(2,1)} %bitcast.178) | data formatting | bytes 33554432
  632.0 11.9 %fusion.33 = f32[128,8,128]{0,2,1:T(8,128)} fusion(pred[128,8192]{1,0:T(8,128)(4,1)S(1)} %iota_compare_fusion.1, bf16[8,8192]{1,0:T(8,128)(2,1)} %bitcast.193, bf16[8192,8,128]{2,1,0:T(8,128)(2,1)} %bitcast.184, f32[128,8]{0,1:T(8,128)S(1)} %convolution_add_fusion, f32[8]{0:T(128)S(1)} %copy-done.9), kind=kOutput, calls=%fused_computation.57 | convolution fusion | flops 2156134400 | bytes 18485280 | tf_op jit(solution)/shard_map/hqs,shd->qhd/dot_general | solution.py:166
  643.9 1.7 fusion.38
  645.6 2.8 convolution_convert_fusion
  (134 shorter events, 25.1 us)
Async XLA Ops:
  6.5 35.3 %copy-start = (bf16[1024,1024]{1,0:T(8,128)(2,1)S(1)}, bf16[1024,1024]{1,0:T(8,128)(2,1)}, u32[]{:S(2)}) copy-start(bf16[1024,1024]{1,0:T(8,128)(2,1)} %param.18) | copy-start | bytes 6291460
  6.5 339.7 %all-gather.3.cloned.1.call-start = ((), (), s32[]{:S(2)}) async-start(), calls=%async_computation.2 | async-start | bytes 2359296 | tf_op jit(solution)/shard_map/all_gather | solution.py:82
  27.7 14.0 %all-to-all-start = ((s32[8,1,1024]{2,1,0:T(1,128)}), s32[8,1,1024]{2,1,0:T(1,128)S(1)}, u32[]{:S(2)}, u32[]{:S(2)}) async-start(s32[8,1,1024]{2,1,0:T(1,128)} %bitcast.9), calls=%async_computation | async-start | bytes 65536 | tf_op jit(solution)/shard_map/all_to_all | solution.py:135
  34.9 610.7 %all-gather.5.cloned.1.call-start = ((), (), s32[]{:S(2)}) async-start(), calls=%async_computation.3 | async-start | bytes 2621440 | tf_op jit(solution)/shard_map/all_gather | solution.py:181
  38.3 0.8 copy-start.3
  77.3 27.0 %copy-start.2 = (bf16[1024,1024]{1,0:T(8,128)(2,1)S(1)}, bf16[1024,1024]{1,0:T(8,128)(2,1)}, u32[]{:S(2)}) copy-start(bf16[1024,1024]{1,0:T(8,128)(2,1)} %param.17) | copy-start | bytes 6291460
  88.3 82.4 %collective-permute-start = (bf16[1,1,1024,1024]{3,2,0,1:T(8,128)(2,1)}, bf16[1,1,1024,1024]{3,2,0,1:T(8,128)(2,1)}, u32[]{:S(2)}, u32[]{:S(2)}) collective-permute-start(bf16[1,1,1024,1024]{3,2,0,1:T(8,128)(2,1)} %get-tuple-element.212), channel_id=1, source_target_pairs={{0,4},{4,8},{8,12},{12,16},{16,20},{20,24},{24,28},{28,0},{1,5},{5... | collective-permute-start | bytes 6291464 | tf_op jit(solution)/shard_map/ppermute | solution.py:36
  104.3 6.5 copy-start.4
  111.7 63.6 %collective-permute-start.1 = (bf16[1,1,1024,1024]{3,2,0,1:T(8,128)(2,1)}, bf16[1,1,1024,1024]{3,2,0,1:T(8,128)(2,1)}, u32[]{:S(2)}, u32[]{:S(2)}) collective-permute-start(bf16[1,1,1024,1024]{3,2,0,1:T(8,128)(2,1)} %get-tuple-element.211), channel_id=1, source_target_pairs={{0,8},{4,12},{8,16},{12,20},{16,24},{20,28},{24,0},{28,4},{1,9},{5... | collective-permute-start | bytes 6291464 | tf_op jit(solution)/shard_map/ppermute | solution.py:36
  112.9 204.2 %collective-permute-start.2 = (bf16[1,1,1024,1024]{3,2,0,1:T(8,128)(2,1)}, bf16[1,1,1024,1024]{3,2,0,1:T(8,128)(2,1)}, u32[]{:S(2)}, u32[]{:S(2)}) collective-permute-start(bf16[1,1,1024,1024]{3,2,0,1:T(8,128)(2,1)} %get-tuple-element.210), channel_id=1, source_target_pairs={{0,12},{4,16},{8,20},{12,24},{16,28},{20,0},{24,4},{28,8},{1,13},{... | collective-permute-start | bytes 6291464 | tf_op jit(solution)/shard_map/ppermute | solution.py:36
  115.3 224.7 %collective-permute-start.3 = (bf16[1,1,1024,1024]{3,2,0,1:T(8,128)(2,1)}, bf16[1,1,1024,1024]{3,2,0,1:T(8,128)(2,1)}, u32[]{:S(2)}, u32[]{:S(2)}) collective-permute-start(bf16[1,1,1024,1024]{3,2,0,1:T(8,128)(2,1)} %get-tuple-element.209), channel_id=1, source_target_pairs={{0,16},{4,20},{8,24},{12,28},{16,0},{20,4},{24,8},{28,12},{1,17},{... | collective-permute-start | bytes 6291464 | tf_op jit(solution)/shard_map/ppermute | solution.py:36
  116.9 226.3 %collective-permute-start.4 = (bf16[1,1,1024,1024]{3,2,0,1:T(8,128)(2,1)}, bf16[1,1,1024,1024]{3,2,0,1:T(8,128)(2,1)}, u32[]{:S(2)}, u32[]{:S(2)}) collective-permute-start(bf16[1,1,1024,1024]{3,2,0,1:T(8,128)(2,1)} %get-tuple-element.208), channel_id=1, source_target_pairs={{0,20},{4,24},{8,28},{12,0},{16,4},{20,8},{24,12},{28,16},{1,21},{... | collective-permute-start | bytes 6291464 | tf_op jit(solution)/shard_map/ppermute | solution.py:36
  170.7 438.7 %collective-permute-start.5 = (bf16[1,1,1024,1024]{3,2,0,1:T(8,128)(2,1)}, bf16[1,1,1024,1024]{3,2,0,1:T(8,128)(2,1)}, u32[]{:S(2)}, u32[]{:S(2)}) collective-permute-start(bf16[1,1,1024,1024]{3,2,0,1:T(8,128)(2,1)} %get-tuple-element.213), channel_id=1, source_target_pairs={{0,24},{4,28},{8,0},{12,4},{16,8},{20,12},{24,16},{28,20},{1,25},{... | collective-permute-start | bytes 6291464 | tf_op jit(solution)/shard_map/ppermute | solution.py:36
  175.3 437.2 %collective-permute-start.6 = (bf16[1,1,1024,1024]{3,2,0,1:T(8,128)(2,1)}, bf16[1,1,1024,1024]{3,2,0,1:T(8,128)(2,1)}, u32[]{:S(2)}, u32[]{:S(2)}) collective-permute-start(bf16[1,1,1024,1024]{3,2,0,1:T(8,128)(2,1)} %get-tuple-element.207), channel_id=1, source_target_pairs={{0,28},{4,0},{8,4},{12,8},{16,12},{20,16},{24,20},{28,24},{1,29},{... | collective-permute-start | bytes 6291464 | tf_op jit(solution)/shard_map/ppermute | solution.py:36
  603.5 27.8 %all-to-all-start.1 = ((bf16[8,1024,8]{1,2,0:T(8,128)(2,1)}), bf16[8,1024,8]{1,2,0:T(8,128)(2,1)S(1)}, u32[]{:S(2)}, u32[]{:S(2)}) async-start(bf16[8,1024,8]{1,2,0:T(8,128)(2,1)} %get-tuple-element.101), calls=%async_computation.1 | async-start | bytes 262144 | tf_op jit(solution)/shard_map/all_to_all | solution.py:160
  615.6 16.4 %copy-start.9 = (f32[8]{0:T(128)S(1)}, f32[8]{0:T(128)}, u32[]{:S(2)}) copy-start(f32[8]{0:T(128)} %get-tuple-element.202) | copy-start | bytes 100
  631.2 0.7 copy-start.6
  632.0 11.9 %copy-start.5 = (bf16[128,1024]{0,1:T(8,128)(2,1)S(1)}, bf16[128,1024]{0,1:T(8,128)(2,1)}, u32[]{:S(2)}) copy-start(bf16[128,1024]{0,1:T(8,128)(2,1)} %copy.77) | copy-start | bytes 786436
  632.0 11.9 %copy-start.7 = (f32[8,128]{1,0:T(8,128)S(1)}, f32[8,128]{1,0:T(8,128)}, u32[]{:S(2)}) copy-start(f32[8,128]{1,0:T(8,128)} %fusion.64) | copy-start | bytes 12292
  632.0 11.9 %copy-start.8 = (f32[8]{0:T(128)S(1)}, f32[8]{0:T(128)}, u32[]{:S(2)}) copy-start(f32[8]{0:T(128)} %get-tuple-element.201) | copy-start | bytes 100
  632.0 16.4 %copy-start.1 = (bf16[1024,1024]{1,0:T(8,128)(2,1)S(1)}, bf16[1024,1024]{1,0:T(8,128)(2,1)}, u32[]{:S(2)}) copy-start(bf16[1024,1024]{1,0:T(8,128)(2,1)} %param.18) | copy-start | bytes 6291460
Sparse Core Ops, SparseCore 0:
  9.5 51.9 all-gather.2
  63.1 21.0 all-gather.4
